TPU v7x, 256 devices: a whole 4x4x8 slice. The times are simulated.
256 devices in a mesh: dp: 16 (over y_hi, x, core), mp: 16 (over y_lo, z).
Axes of the slice: x: 4, y: 4 (y_hi: 2, y_lo: 2; y = y_hi * 2 + y_lo), z: 8, core: 2. Of those that a mesh axis runs over, the one named last changes fastest.
Arguments:
- activations: bfloat16 [4096, 4096], P('dp', 'mp'), may hold values from -6 to 6
- output_grads: bfloat16 [4096, 32768], P('dp', 'mp'), may hold values from -0.09375 to 0.09375
- owners: int32 [16, 16], replicated, may hold values from 0 to 15, as said below
- statistics: float32 [16, 16, 1024, 1024], P('mp', 'dp'), may hold values from -3 to 8
- inv_roots: bfloat16 [16, 16, 1024, 1024], P('mp', 'dp'), may hold values from -3 to 6
Outputs:
- new_statistics: float32 [16, 16, 1024, 1024], P('mp', 'dp')
- preconditioned: bfloat16 [4096, 32768], P('dp', 'mp')
Inputs may be any that keep to these rules, and one draw needn't show every extreme that they name: `owners`: each row holds every number of 0 to 15 once; entries 2b and 2b + 1 are 2k and 2k + 1 in some order, for some k.
All inputs are finite; a program needn't handle non-finite values.
Results may differ from a plain program's by a relative error of at most 0.024.
Values may be sent and summed in bfloat16 or wider, within the bound.
No kernel may reach another device: no remote copies, remote signals or barrier semaphores. Data moves between devices by JAX's collectives and lax.ppermute only.
A program may use at most 128 MiB of HBM per device.

v0:
```python
import jax
import jax.numpy as jnp
from jax import lax
from jax.sharding import PartitionSpec as P

D = 4096
BLK = 1024
decay_rate = 0.9


def from_partner(x, axis, distance):
    return lax.ppermute(x, axis, [(i, i ^ 1 << distance) for i in range(lax.axis_size(axis))])


def owner_layout(owner_table, devices):
    mp_index = lax.axis_index("mp")
    table_row = lax.dynamic_index_in_dim(owner_table, mp_index, 0, keepdims=False)
    slots = jnp.arange(devices, dtype=jnp.int32)
    match = (table_row[None, :] == slots[:, None]).astype(jnp.int32)
    position = jnp.sum(match * slots[None, :], axis=1)
    return (table_row, position)


def on_device(activations, output_grads, owners, statistics, inv_roots):
    devices = lax.axis_size("dp")
    col_blocks = output_grads.shape[1] // BLK
    half_rows = BLK // 2
    rows_dev = D // devices
    table_row, position = owner_layout(owners, devices)
    my_index = lax.axis_index("dp")
    my_position = position[my_index]
    left_side = my_position % 2 == 0
    my_block = my_position // 2
    parity = my_index % 2
    all_features = lax.all_gather(activations, "mp", axis=1, tiled=True)
    owner_ids = jnp.arange(devices, dtype=jnp.int32)
    owner_block = position // 2
    owner_rows = owner_block // col_blocks * BLK + owner_ids % 2 * half_rows
    owner_cols = owner_block % col_blocks * BLK

    def select_parts(owner_index):
        feature_part = lax.dynamic_slice_in_dim(all_features, owner_rows[owner_index], half_rows, 1)
        grad_part = lax.dynamic_slice_in_dim(output_grads, owner_cols[owner_index], BLK, 1)
        return (feature_part, grad_part)

    def owner_term(owner_index):
        feature_part, grad_part = select_parts(owner_index)
        return lax.dot_general(
            feature_part, grad_part, (((0,), (0,)), ((), ())), preferred_element_type=jnp.float32
        )

    picked = jnp.arange(half_rows * lax.axis_size("dp") // half_rows, dtype=jnp.int32)
    summed = lax.psum_scatter(
        jax.vmap(owner_term)(picked)
        .reshape(half_rows * lax.axis_size("dp"), BLK)
        .astype(jnp.bfloat16),
        "dp",
        scatter_dimension=0,
        tiled=True,
    )
    other_half = from_partner(summed, "dp", 0)
    block_grad = jnp.where(
        parity == 0,
        jnp.concatenate([summed, other_half], 0),
        jnp.concatenate([other_half, summed], 0),
    )
    old_stat = statistics[0, 0]
    gram_matrix = lax.cond(
        left_side,
        lambda: lax.dot_general(
            block_grad, block_grad, (((1,), (1,)), ((), ())), preferred_element_type=jnp.float32
        ),
        lambda: lax.dot_general(
            block_grad, block_grad, (((0,), (0,)), ((), ())), preferred_element_type=jnp.float32
        ),
    )
    new_stat = decay_rate * old_stat + (1.0 - decay_rate) / BLK * gram_matrix
    own_root = inv_roots[0, 0]
    payload = lax.cond(
        left_side,
        lambda: jnp.dot(own_root, block_grad, preferred_element_type=jnp.float32).astype(
            jnp.bfloat16
        ),
        lambda: own_root,
    )
    received = from_partner(payload, "dp", 0)
    left_product = jnp.where(left_side, payload, received)
    right_root = jnp.where(left_side, received, own_root)
    columns = lax.dynamic_slice_in_dim(right_root, parity * half_rows, half_rows, 1)
    result_part = jnp.dot(left_product, columns, preferred_element_type=jnp.float32).astype(
        jnp.bfloat16
    )
    block_row = my_block // col_blocks
    row_block = my_index * rows_dev // BLK
    pair_bases = 2 * (table_row[0::2] // 2)
    wanted = row_block * col_blocks + jnp.arange(col_blocks, dtype=jnp.int32)
    sources = (
        jnp.take(pair_bases, wanted)[:, None] + jnp.arange(2, dtype=jnp.int32)[None, :]
    ).reshape(-1)
    pieces = result_part.reshape(BLK // rows_dev, rows_dev, half_rows)
    outgoing = jnp.zeros((devices, rows_dev, half_rows), jnp.bfloat16)
    outgoing = lax.dynamic_update_slice_in_dim(outgoing, pieces, block_row * (BLK // rows_dev), 0)
    incoming = lax.all_to_all(outgoing, "dp", split_axis=0, concat_axis=2, tiled=True)
    incoming = incoming.reshape(rows_dev, devices, half_rows)
    gathered = jnp.take(incoming, sources, axis=1)
    preconditioned = gathered.reshape(rows_dev, col_blocks * BLK)
    return (new_stat[None, None], preconditioned)


def solution(mesh):
    in_specs = (
        P("dp", "mp"),
        P("dp", "mp"),
        P(),
        P("mp", "dp", None, None),
        P("mp", "dp", None, None),
    )
    out_specs = (P("mp", "dp", None, None), P("dp", "mp"))
    return jax.shard_map(
        on_device, mesh=mesh, in_specs=in_specs, out_specs=out_specs, check_vma=False
    )
```

profile of v0, /device:TPU:2, one launch (start us, length us, event | category | flops | bytes accessed | tf_op | source)
XLA Modules:
  0.0 399.0 jit_solution(15943701818986518734)
XLA Ops:
  9.5 53.0 %while.3 = (s32[]{:T(128)}, bf16[256,2048]{1,0:T(8,128)(2,1)}, s32[16,2]{0,1:T(2,128)S(1)}, bf16[16,256,1024]{2,1,0:T(8,128)(2,1)}, s32[]{:T(128)}) while((s32[]{:T(128)}, bf16[256,2048]{1,0:T(8,128)(2,1)}, s32[16,2]{0,1:T(2,128)S(1)}, bf16[16,256,1024]{2,1,0:T(8,128)(2,1)}, s32[]{:T(128)}) %tuple.48), condition=%wide.while_cond.1, body=%wide.while_body.1.sunk | while | flops 2 | bytes 1049689 | solution.py:43
  16.8 2.7 bitcast_dynamic-update-slice_fusion.5
  23.4 2.7 bitcast_dynamic-update-slice_fusion.5
  26.7 2.7 bitcast_dynamic-update-slice_fusion.5
  36.7 2.7 bitcast_dynamic-update-slice_fusion.5
  40.0 2.7 bitcast_dynamic-update-slice_fusion.5
  43.3 2.7 bitcast_dynamic-update-slice_fusion.5
  46.7 2.7 bitcast_dynamic-update-slice_fusion.5
  59.9 2.7 bitcast_dynamic-update-slice_fusion.5
  62.6 22.1 %all-gather.2.cloned.1.call-done = bf16[256,4096]{1,0:T(8,128)(2,1)} async-done(((bf16[256,256]{1,0:T(8,128)(2,1)}), bf16[256,4096]{1,0:T(8,128)(2,1)}) %all-gather.2.cloned.1.call-update) | async-done | bytes 2097168 | tf_op jit(solution)/shard_map/all_gather | solution.py:35
  87.1 48.7 %while.2 = (s32[]{:T(128)}, bf16[256,4096]{1,0:T(8,128)(2,1)}, s32[16,2]{0,1:T(2,128)S(1)}, bf16[16,256,512]{2,1,0:T(8,128)(2,1)}, s32[]{:T(128)}) while((s32[]{:T(128)}, bf16[256,4096]{1,0:T(8,128)(2,1)}, s32[16,2]{0,1:T(2,128)S(1)}, bf16[16,256,512]{2,1,0:T(8,128)(2,1)}, s32[]{:T(128)}) %tuple.45), condition=%wide.while_cond, body=%wide.while_body.sunk | while | flops 2 | bytes 525401 | solution.py:42
  135.8 12.2 %convolution_convert_fusion.1 = bf16[16,512,1024]{2,1,0:T(8,128)(2,1)} fusion(bf16[16,256,512]{2,1,0:T(8,128)(2,1)} %get-tuple-element.24, bf16[16,256,1024]{2,1,0:T(8,128)(2,1)} %get-tuple-element.32), kind=kOutput, calls=%fused_computation.9 | convolution fusion | flops 4303355904 | bytes 29360128 | tf_op jit(solution)/shard_map/vmap()/dot_general | solution.py:48
  148.0 153.9 %reduce-scatter.2.cloned.1.call-done = bf16[512,1024]{1,0:T(8,128)(2,1)} async-done(((bf16[8192,1024]{1,0:T(8,128)(2,1)}), bf16[512,1024]{1,0:T(8,128)(2,1)}) %reduce-scatter.2.cloned.1.call-update) | async-done | bytes 1048592 | tf_op jit(solution)/shard_map/reduce_scatter | solution.py:53
  304.7 3.9 maximum_select_fusion
  308.6 5.3 %conditional.3 = (bf16[1024,1024]{1,0:T(8,128)(2,1)}) conditional(s32[]{:T(128)} %convert_element_type.17, bf16[1024,1024]{1,0:T(8,128)(2,1)S(1)} %bitcast.56, (bf16[1024,1024]{1,0:T(8,128)(2,1)S(1)}, bf16[1024,1024]{1,0:T(8,128)(2,1)}) %tuple.59), branch_computations={%region_4.5_spmd, %region_5.6_spmd} | conditional | flops 2148532224 | bytes 6291464 | solution.py:79
  308.6 5.3 %convolution_convert_fusion = bf16[1024,1024]{1,0:T(8,128)(2,1)} fusion(bf16[1024,1024]{1,0:T(8,128)(2,1)S(1)} %get-tuple-element.13, bf16[1024,1024]{1,0:T(8,128)(2,1)} %get-tuple-element.14), kind=kOutput, calls=%fused_computation.4 | convolution fusion | flops 2148532224 | bytes 6291456 | tf_op jit(solution)/shard_map/cond/branch_1_fun/dot_general | solution.py:81
  314.6 3.8 collective-permute-done.1
  318.4 3.2 fusion.4
  325.1 6.2 %all-to-all-start = ((bf16[16,256,512]{2,1,0:T(8,128)(2,1)}), bf16[16,256,512]{2,1,0:T(8,128)(2,1)}, u32[]{:S(2)}, u32[]{:S(2)}) async-start(bf16[16,256,512]{2,1,0:T(8,128)(2,1)} %constant_dynamic-update-slice_fusion), calls=%async_computation.1 | async-start | bytes 8388608 | tf_op jit(solution)/shard_map/all_to_all | solution.py:103
  332.3 4.6 %conditional.2 = (f32[1024,1024]{1,0:T(8,128)}) conditional(s32[]{:T(128)} %convert_element_type.17, bf16[1024,1024]{1,0:T(8,128)(2,1)S(1)} %copy-done.3, bf16[1024,1024]{1,0:T(8,128)(2,1)S(1)} %copy-done.3), branch_computations={%region_2.3_spmd, %region_3.4_spmd} | conditional | flops 2147483648 | bytes 6291464 | solution.py:68
  332.5 4.4 %fusion.18 = f32[1024,1024]{1,0:T(8,128)} fusion(bf16[1024,1024]{1,0:T(8,128)(2,1)S(1)} %param.1), kind=kOutput, calls=%fused_computation.61 | convolution fusion | flops 2147483648 | bytes 6291456 | tf_op jit(solution)/shard_map/cond/branch_1_fun/dot_general | solution.py:70
  336.9 7.0 %fusion = f32[1,1,1024,1024]{3,2,1,0:T(8,128)} fusion(f32[1024,1024]{1,0:T(8,128)} %get-tuple-element.131, f32[1,1,1024,1024]{3,2,1,0:T(8,128)} %param.12), kind=kLoop, calls=%fused_computation.11 | loop fusion | flops 3145728 | bytes 12582912 | tf_op jit(solution)/shard_map/broadcast_in_dim | solution.py:107
  343.9 44.2 %all-to-all-done = bf16[16,256,512]{2,1,0:T(8,128)(2,1)} async-done(((bf16[16,256,512]{2,1,0:T(8,128)(2,1)}), bf16[16,256,512]{2,1,0:T(8,128)(2,1)}, u32[]{:S(2)}, u32[]{:S(2)}) %all-to-all-start) | async-done | bytes 4194336 | tf_op jit(solution)/shard_map/all_to_all | solution.py:103
  388.1 2.8 gather_fusion.3
  (136 shorter events, 91.3 us)
Async XLA Ops:
  7.2 0.8 copy-start
  7.2 77.5 %all-gather.2.cloned.1.call-start = ((), (), s32[]{:S(2)}) async-start(), calls=%async_computation.2 | async-start | bytes 2228224 | tf_op jit(solution)/shard_map/all_gather | solution.py:35
  7.9 294.0 %reduce-scatter.2.cloned.1.call-start = ((), (), s32[]{:S(2)}) async-start(), calls=%async_computation.3 | async-start | bytes 17825792 | tf_op jit(solution)/shard_map/reduce_scatter | solution.py:53
  148.0 160.6 %copy-start.2 = (bf16[1,1,1024,1024]{3,2,1,0:T(8,128)(2,1)S(1)}, bf16[1,1,1024,1024]{3,2,1,0:T(8,128)(2,1)}, u32[]{:S(2)}) copy-start(bf16[1,1,1024,1024]{3,2,1,0:T(8,128)(2,1)} %param.13) | copy-start | bytes 6291460
  301.9 2.9 collective-permute-start
  313.9 4.5 %collective-permute-start.1 = (bf16[1024,1024]{1,0:T(8,128)(2,1)}, bf16[1024,1024]{1,0:T(8,128)(2,1)}, u32[]{:S(2)}, u32[]{:S(2)}) collective-permute-start(bf16[1024,1024]{1,0:T(8,128)(2,1)} %get-tuple-element.132), channel_id=1, source_target_pairs={{0,16},{16,0},{32,48},{48,32},{64,80},{80,64},{96,112},{112,96},{1... | collective-permute-start | bytes 6291464 | tf_op jit(solution)/shard_map/ppermute | solution.py:12
  325.1 7.3 %copy-start.3 = (bf16[1024,1024]{1,0:T(8,128)(2,1)S(1)}, bf16[1024,1024]{1,0:T(8,128)(2,1)}, u32[]{:S(2)}) copy-start(bf16[1024,1024]{1,0:T(8,128)(2,1)} %maximum_select_fusion) | copy-start | bytes 6291460
  325.1 63.1 %all-to-all-start = ((bf16[16,256,512]{2,1,0:T(8,128)(2,1)}), bf16[16,256,512]{2,1,0:T(8,128)(2,1)}, u32[]{:S(2)}, u32[]{:S(2)}) async-start(bf16[16,256,512]{2,1,0:T(8,128)(2,1)} %constant_dynamic-update-slice_fusion), calls=%async_computation.1 | async-start | bytes 8388608 | tf_op jit(solution)/shard_map/all_to_all | solution.py:103
  336.9 55.2 %copy-start.1 = (s32[16,16]{1,0:T(8,128)S(1)}, s32[16,16]{1,0:T(8,128)}, u32[]{:S(2)}) copy-start(s32[16,16]{1,0:T(8,128)} %param.11) | copy-start | bytes 3076
Sparse Core Ops, SparseCore 0:
  9.7 74.9 all-gather.1
  148.1 153.6 reduce-scatter.1
where the time goes:
time: 401 us; the launch traced here: 399 us
  waiting for transfers between devices  225 us (56%)
  local copies, waits for them, and re-layouts  113 us (28%)
  matrix products  25 us (6%)
  between operations  16.9 us (4%)
  other arithmetic  12.2 us (3%)
  starting transfers between devices  6.23 us (2%)
    reduce_scatter x1, waiting for transfers between devices, on_device(): lax.psum_scatter(jax.vmap(owner_term)(picked).reshape(half_rows * lax.axi...  154 us
    gather x96, local copies, waits for them, and re-layouts  102 us
    all_to_all x1, waiting for transfers between devices, on_device(): lax.all_to_all(outgoing, 'dp', split_axis=0, concat_axis=2, tiled=True)  44.2 us
    all_gather x1, waiting for transfers between devices, on_device(): all_features = lax.all_gather(activations, 'mp', axis=1, tiled=True)  22.1 us
    dot_general x1, matrix products, owner_term(): lax.dot_general(feature_part, grad_part, (((0,), (0,)), ((), ())), prefer...  12.2 us
  transfers between devices with their start and end apart: 5, of which 5 were waited for; matrix products, arithmetic and copies ran while one was open for 17% of the time, Pallas kernels for 0%

commit v1 on v0

--- a/solution.py
+++ b/solution.py
@@ -32,7 +32,9 @@
     left_side = my_position % 2 == 0
     my_block = my_position // 2
     parity = my_index % 2
-    all_features = lax.all_gather(activations, "mp", axis=1, tiled=True)
+    all_features = jnp.concatenate(
+        lax.all_to_all(jnp.stack([activations] * lax.axis_size("mp")), "mp", 0, 0), axis=1
+    )
     owner_ids = jnp.arange(devices, dtype=jnp.int32)
     owner_block = position // 2
     owner_rows = owner_block // col_blocks * BLK + owner_ids % 2 * half_rows

time: 401 us -> 386 us (0.963)
  waiting for transfers between devices: 225 us -> 212 us
  local copies, waits for them, and re-layouts: 113 us -> 103 us
  starting transfers between devices: 6.23 us -> 15.8 us
    all_gather x1 -> x0, waiting for transfers between devices: 22.1 us -> none  [on_device(): all_features = lax.all_gather(activations, 'mp', axis=1, tiled=True)]
    gather x96 -> x128, local copies, waits for them, and re-layouts: 102 us -> 86.2 us
    all_to_all x0 -> x1, waiting for transfers between devices: none -> 10.8 us  [on_device(): lax.all_to_all(jnp.stack([activations] * lax.axis_size('mp')), 'mp', 0, 0)]
    all_to_all x0 -> x1, starting transfers between devices: none -> 9.58 us  [on_device(): lax.all_to_all(jnp.stack([activations] * lax.axis_size('mp')), 'mp', 0, 0)]
  transfers between devices with their start and end apart: 5 -> 5, of which waited for: 5 -> 5; matrix products, arithmetic and copies ran while one was open for 17% -> 13% of each run, Pallas kernels for 0% -> 0%
where the time goes in v1:
time: 386 us; the launch traced here: 385 us
  waiting for transfers between devices  212 us (55%)
  local copies, waits for them, and re-layouts  103 us (27%)
  matrix products  25 us (6%)
  between operations  16.9 us (4%)
  starting transfers between devices  15.8 us (4%)
  other arithmetic  12.2 us (3%)
    reduce_scatter x1, waiting for transfers between devices, on_device(): lax.psum_scatter(jax.vmap(owner_term)(picked).reshape(half_rows * lax.axi...  153 us
    gather x128, local copies, waits for them, and re-layouts  86.2 us
    all_to_all x1, waiting for transfers between devices, on_device(): lax.all_to_all(outgoing, 'dp', split_axis=0, concat_axis=2, tiled=True)  44.2 us
    dot_general x1, matrix products, owner_term(): lax.dot_general(feature_part, grad_part, (((0,), (0,)), ((), ())), prefer...  12.2 us
    all_to_all x1, waiting for transfers between devices, on_device(): lax.all_to_all(jnp.stack([activations] * lax.axis_size('mp')), 'mp', 0, 0)  10.8 us
    all_to_all x1, starting transfers between devices, on_device(): lax.all_to_all(jnp.stack([activations] * lax.axis_size('mp')), 'mp', 0, 0)  9.58 us
  transfers between devices with their start and end apart: 5, of which 5 were waited for; matrix products, arithmetic and copies ran while one was open for 13% of the time, Pallas kernels for 0%

profile of v1, /device:TPU:2, one launch (start us, length us, event | category | flops | bytes accessed | tf_op | source)
XLA Modules:
  0.0 385.1 jit_solution(13073659282532014347)
XLA Ops:
  7.2 2.5 stack.2
  9.7 9.6 %all-to-all-start = ((bf16[16,256,256]{2,1,0:T(8,128)(2,1)}), bf16[16,256,256]{2,1,0:T(8,128)(2,1)S(1)}, u32[]{:S(2)}, u32[]{:S(2)}) async-start(bf16[16,256,256]{2,1,0:T(8,128)(2,1)} %stack.2), calls=%async_computation | async-start | bytes 4194304 | tf_op jit(solution)/shard_map/all_to_all | solution.py:36
  20.9 36.6 %while.3 = (s32[]{:T(128)}, bf16[256,2048]{1,0:T(8,128)(2,1)S(1)}, s32[16,2]{0,1:T(2,128)S(1)}, bf16[16,256,1024]{2,1,0:T(8,128)(2,1)}, s32[]{:T(128)}) while((s32[]{:T(128)}, bf16[256,2048]{1,0:T(8,128)(2,1)S(1)}, s32[16,2]{0,1:T(2,128)S(1)}, bf16[16,256,1024]{2,1,0:T(8,128)(2,1)}, s32[]{:T(128)}) %tuple.59), condition=%wide.while_cond.1, body=%wide.while_body.1.sunk | while | flops 2 | bytes 1049689 | solution.py:45
  26.1 1.7 bitcast_dynamic-update-slice_fusion.5
  44.4 1.7 bitcast_dynamic-update-slice_fusion.5
  55.8 1.7 bitcast_dynamic-update-slice_fusion.5
  57.5 10.8 %all-to-all-done = bf16[16,256,256]{2,1,0:T(8,128)(2,1)S(1)} async-done(((bf16[16,256,256]{2,1,0:T(8,128)(2,1)}), bf16[16,256,256]{2,1,0:T(8,128)(2,1)S(1)}, u32[]{:S(2)}, u32[]{:S(2)}) %all-to-all-start) | async-done | bytes 2097184 | tf_op jit(solution)/shard_map/all_to_all | solution.py:36
  68.3 2.4 copy.17
  70.7 2.4 broadcast.206.clone
  73.1 49.9 %while.2 = (s32[]{:T(128)}, bf16[256,4096]{0,1:T(8,128)(2,1)}, s32[16,2]{0,1:T(2,128)S(1)}, bf16[16,256,512]{2,1,0:T(8,128)(2,1)}, s32[]{:T(128)}) while((s32[]{:T(128)}, bf16[256,4096]{0,1:T(8,128)(2,1)}, s32[16,2]{0,1:T(2,128)S(1)}, bf16[16,256,512]{2,1,0:T(8,128)(2,1)}, s32[]{:T(128)}) %tuple.60), condition=%wide.while_cond, body=%wide.while_body.sunk | while | flops 2 | bytes 1573469 | solution.py:44
  123.0 12.2 %convolution_convert_fusion.1 = bf16[16,512,1024]{2,1,0:T(8,128)(2,1)} fusion(bf16[16,256,512]{2,1,0:T(8,128)(2,1)} %get-tuple-element.24, bf16[16,256,1024]{2,1,0:T(8,128)(2,1)} %get-tuple-element.32), kind=kOutput, calls=%fused_computation.10 | convolution fusion | flops 4303355904 | bytes 29360128 | tf_op jit(solution)/shard_map/vmap()/dot_general | solution.py:50
  135.2 152.8 %reduce-scatter.2.cloned.1.call-done = bf16[512,1024]{1,0:T(8,128)(2,1)} async-done(((bf16[8192,1024]{1,0:T(8,128)(2,1)}), bf16[512,1024]{1,0:T(8,128)(2,1)}) %reduce-scatter.2.cloned.1.call-update) | async-done | bytes 1048592 | tf_op jit(solution)/shard_map/reduce_scatter | solution.py:55
  290.8 3.9 %maximum_select_fusion = bf16[1024,1024]{1,0:T(8,128)(2,1)} fusion(bf16[512,1024]{1,0:T(8,128)(2,1)S(1)} %collective-permute-done, bf16[512,1024]{1,0:T(8,128)(2,1)} %reduce-scatter.2.cloned.1.call-done, pred[]{:T(512)S(6)} %eq.32), kind=kLoop, calls=%fused_computation.13 | loop fusion | flops 9437184 | bytes 4194305 | tf_op jit(solution)/shard_map/jit(_where)/select_n | solution.py:64
  294.8 5.3 %conditional.3 = (bf16[1024,1024]{1,0:T(8,128)(2,1)}) conditional(s32[]{:T(128)} %convert_element_type.17, bf16[1024,1024]{1,0:T(8,128)(2,1)S(1)} %bitcast.60, (bf16[1024,1024]{1,0:T(8,128)(2,1)S(1)}, bf16[1024,1024]{1,0:T(8,128)(2,1)}) %tuple.61), branch_computations={%region_4.5_spmd, %region_5.6_spmd} | conditional | flops 2148532224 | bytes 6291464 | solution.py:81
  294.8 5.3 %convolution_convert_fusion = bf16[1024,1024]{1,0:T(8,128)(2,1)} fusion(bf16[1024,1024]{1,0:T(8,128)(2,1)S(1)} %get-tuple-element.13, bf16[1024,1024]{1,0:T(8,128)(2,1)} %get-tuple-element.14), kind=kOutput, calls=%fused_computation.4 | convolution fusion | flops 2148532224 | bytes 6291456 | tf_op jit(solution)/shard_map/cond/branch_1_fun/dot_general | solution.py:83
  300.7 3.8 collective-permute-done.1
  304.5 3.2 fusion.4
  307.7 2.4 broadcast.206
  311.2 6.2 %all-to-all-start.1 = ((bf16[16,256,512]{2,1,0:T(8,128)(2,1)}), bf16[16,256,512]{2,1,0:T(8,128)(2,1)}, u32[]{:S(2)}, u32[]{:S(2)}) async-start(bf16[16,256,512]{2,1,0:T(8,128)(2,1)} %constant_dynamic-update-slice_fusion), calls=%async_computation.2 | async-start | bytes 8388608 | tf_op jit(solution)/shard_map/all_to_all | solution.py:105
  318.5 4.6 %conditional.2 = (f32[1024,1024]{1,0:T(8,128)}) conditional(s32[]{:T(128)} %convert_element_type.17, bf16[1024,1024]{1,0:T(8,128)(2,1)S(1)} %copy-done.4, bf16[1024,1024]{1,0:T(8,128)(2,1)S(1)} %copy-done.4), branch_computations={%region_2.3_spmd, %region_3.4_spmd} | conditional | flops 2147483648 | bytes 6291464 | solution.py:70
  318.7 4.4 %fusion.18 = f32[1024,1024]{1,0:T(8,128)} fusion(bf16[1024,1024]{1,0:T(8,128)(2,1)S(1)} %param.1), kind=kOutput, calls=%fused_computation.62 | convolution fusion | flops 2147483648 | bytes 6291456 | tf_op jit(solution)/shard_map/cond/branch_1_fun/dot_general | solution.py:72
  323.1 7.0 %fusion = f32[1,1,1024,1024]{3,2,1,0:T(8,128)} fusion(f32[1024,1024]{1,0:T(8,128)} %get-tuple-element.139, f32[1,1,1024,1024]{3,2,1,0:T(8,128)} %param.12), kind=kLoop, calls=%fused_computation.12 | loop fusion | flops 3145728 | bytes 12582912 | tf_op jit(solution)/shard_map/broadcast_in_dim | solution.py:109
  330.0 44.2 %all-to-all-done.1 = bf16[16,256,512]{2,1,0:T(8,128)(2,1)} async-done(((bf16[16,256,512]{2,1,0:T(8,128)(2,1)}), bf16[16,256,512]{2,1,0:T(8,128)(2,1)}, u32[]{:S(2)}, u32[]{:S(2)}) %all-to-all-start.1) | async-done | bytes 4194336 | tf_op jit(solution)/shard_map/all_to_all | solution.py:105
  374.3 2.8 gather_fusion.3
  (171 shorter events, 87.0 us)
Async XLA Ops:
  7.2 12.2 %copy-start = (s32[16,16]{1,0:T(8,128)S(1)}, s32[16,16]{1,0:T(8,128)}, u32[]{:S(2)}) copy-start(s32[16,16]{1,0:T(8,128)} %param.11) | copy-start | bytes 3076
  7.2 13.8 %copy-start.2 = (bf16[256,2048]{1,0:T(8,128)(2,1)S(1)}, bf16[256,2048]{1,0:T(8,128)(2,1)}, u32[]{:S(2)}) copy-start(bf16[256,2048]{1,0:T(8,128)(2,1)} %param.10) | copy-start | bytes 3145732
  9.7 58.6 %all-to-all-start = ((bf16[16,256,256]{2,1,0:T(8,128)(2,1)}), bf16[16,256,256]{2,1,0:T(8,128)(2,1)S(1)}, u32[]{:S(2)}, u32[]{:S(2)}) async-start(bf16[16,256,256]{2,1,0:T(8,128)(2,1)} %stack.2), calls=%async_computation | async-start | bytes 4194304 | tf_op jit(solution)/shard_map/all_to_all | solution.py:36
  19.3 268.7 %reduce-scatter.2.cloned.1.call-start = ((), (), s32[]{:S(2)}) async-start(), calls=%async_computation.3 | async-start | bytes 17825792 | tf_op jit(solution)/shard_map/reduce_scatter | solution.py:55
  135.2 159.6 %copy-start.3 = (bf16[1,1,1024,1024]{3,2,1,0:T(8,128)(2,1)S(1)}, bf16[1,1,1024,1024]{3,2,1,0:T(8,128)(2,1)}, u32[]{:S(2)}) copy-start(bf16[1,1,1024,1024]{3,2,1,0:T(8,128)(2,1)} %param.13) | copy-start | bytes 6291460
  288.0 2.9 collective-permute-start
  300.0 4.5 %collective-permute-start.1 = (bf16[1024,1024]{1,0:T(8,128)(2,1)}, bf16[1024,1024]{1,0:T(8,128)(2,1)}, u32[]{:S(2)}, u32[]{:S(2)}) collective-permute-start(bf16[1024,1024]{1,0:T(8,128)(2,1)} %get-tuple-element.140), channel_id=1, source_target_pairs={{0,16},{16,0},{32,48},{48,32},{64,80},{80,64},{96,112},{112,96},{1... | collective-permute-start | bytes 6291464 | tf_op jit(solution)/shard_map/ppermute | solution.py:12
  311.2 7.3 %copy-start.4 = (bf16[1024,1024]{1,0:T(8,128)(2,1)S(1)}, bf16[1024,1024]{1,0:T(8,128)(2,1)}, u32[]{:S(2)}) copy-start(bf16[1024,1024]{1,0:T(8,128)(2,1)} %maximum_select_fusion) | copy-start | bytes 6291460
  311.2 63.1 %all-to-all-start.1 = ((bf16[16,256,512]{2,1,0:T(8,128)(2,1)}), bf16[16,256,512]{2,1,0:T(8,128)(2,1)}, u32[]{:S(2)}, u32[]{:S(2)}) async-start(bf16[16,256,512]{2,1,0:T(8,128)(2,1)} %constant_dynamic-update-slice_fusion), calls=%async_computation.2 | async-start | bytes 8388608 | tf_op jit(solution)/shard_map/all_to_all | solution.py:105
  323.1 55.2 %copy-start.1 = (s32[16,16]{1,0:T(8,128)S(1)}, s32[16,16]{1,0:T(8,128)}, u32[]{:S(2)}) copy-start(s32[16,16]{1,0:T(8,128)} %param.11) | copy-start | bytes 3076
Sparse Core Ops, SparseCore 0:
  135.3 152.6 reduce-scatter.1
